TPU v7x, 32 devices: a whole 2x2x4 slice. The times are simulated.
32 devices in a mesh: tm: 4 (over y, x), slab: 8 (over z, core).
Axes of the slice: x: 2, y: 2, z: 4, core: 2. Of those that a mesh axis runs over, the one named last changes fastest.
Arguments:
- initial: float32 [4, 16, 64, 16, 128], P('tm', None, 'slab'), may hold values from -6 to 6
- source: float32 [4, 64, 16, 128], P('tm', 'slab'), may hold values from -6 to 6
- decay_rate: float32 [64, 16, 128], P('slab'), may hold values from 0.01 to 0.2
- observed: float32 [4, 16, 64, 16, 128], P('tm', None, 'slab'), may hold values from -6 to 6
- release: int32 [4, 16], replicated, may hold values from 0 to 3
- smooth_taps: float32 [31], replicated, may hold values from 0.02 to 0.08
Outputs:
- source_gradient: float32 [4, 64, 2048], P('tm', None, 'slab')
- decay_gradient: float32 [4, 64, 2048], P('tm', None, 'slab')
All inputs are finite; a program needn't handle non-finite values.
Results may differ from a plain program's by a relative error of at most 0.0003.
Values sent between devices are 32-bit elements; how exact they have to be, the bound alone decides.
A program may use at most 64 MiB of HBM per device.

v0:
```python
import jax
import jax.numpy as jnp
from jax import lax
from jax.sharding import PartitionSpec as P

STEPS = 4


vertical_rate = 0.2
lateral_rate = 0.1


def extended(shard, sides, width):
    for axis, dim in sides:
        peers, length = (lax.axis_size(axis), shard.shape[dim])
        up = [(i, (i + 1) % peers) for i in range(peers - 1)]
        down = [(j, i) for i, j in up]
        last = lax.slice_in_dim(shard, length - width, length, axis=dim)
        first = lax.slice_in_dim(shard, 0, width, axis=dim)
        before = lax.ppermute(last, axis, up)
        after = lax.ppermute(first, axis, down)
        shard = jnp.concatenate([before, shard, after], axis=dim)
    return shard


def shifted(value, axis, steps):
    count = lax.axis_size(axis)
    pairs = [(source, (source + steps) % count) for source in range(count)]
    return lax.ppermute(value, axis, pairs)


def apply_operator(current, decay_rate):
    stretched = extended(current, (("slab", 1),), 1)
    vertical = stretched[:, 2:] + stretched[:, :-2]
    padded = jnp.pad(current, ((0, 0), (0, 0), (1, 1), (1, 1)))
    lateral = padded[:, :, 2:, 1:-1] + padded[:, :, :-2, 1:-1]
    lateral = lateral + padded[:, :, 1:-1, 2:] + padded[:, :, 1:-1, :-2]
    centre = 1.0 - 2.0 * vertical_rate - 4.0 * lateral_rate - decay_rate
    return current * centre + vertical_rate * vertical + lateral_rate * lateral


def smoothing_matrix(smooth_taps, depth):
    count = smooth_taps.shape[0]
    middle = (count - 1) // 2
    rows = jnp.arange(depth, dtype=jnp.int32)[:, None]
    columns = jnp.arange(depth, dtype=jnp.int32)[None, :]
    offset = columns - rows + middle
    match = (offset[:, :, None] == jnp.arange(count, dtype=jnp.int32)[None, None, :]).astype(
        smooth_taps.dtype
    )
    return jnp.sum(match * smooth_taps[None, None, :], axis=-1)


def run_forward(start_field, release_field, release_row, decay_rate):
    states = [start_field]
    current = start_field
    for step_index in range(STEPS):
        chosen = (release_row == step_index).astype(start_field.dtype)
        current = (
            apply_operator(current, decay_rate) + chosen[:, None, None, None] * release_field[None]
        )
        states.append(current)
    return states


def body(initial, source, decay_rate, observed, release, smooth_taps):
    groups = lax.axis_size("tm")
    half_way = groups // 2
    tm_index = lax.axis_index("tm")
    partner_index = (tm_index + half_way) % groups
    partner_release = lax.dynamic_index_in_dim(release, partner_index, 0, keepdims=False)
    start_field = initial[0]
    release_field = source[0]
    partner_start, partner_source = shifted((start_field, release_field), "tm", half_way)
    states = run_forward(partner_start, partner_source, partner_release, decay_rate)
    adjoint = states[STEPS] - observed[0]
    source_grad = jnp.zeros(release_field.shape, jnp.float32)
    decay_grad = jnp.zeros(release_field.shape, jnp.float32)
    for step_index in reversed(range(STEPS)):
        decay_grad = decay_grad - jnp.sum(adjoint * states[step_index], axis=0)
        chosen = (partner_release == step_index).astype(jnp.float32)
        source_grad = source_grad + jnp.sum(chosen[:, None, None, None] * adjoint, axis=0)
        if step_index > 0:
            adjoint = apply_operator(adjoint, decay_rate)
    local_depth = release_field.shape[0]
    depth = local_depth * lax.axis_size("slab")
    matrix = smoothing_matrix(smooth_taps, depth)
    both = jnp.stack([source_grad.reshape(local_depth, -1), decay_grad.reshape(local_depth, -1)])
    smoothed = jnp.einsum(
        "ij,bjk->bik",
        matrix,
        lax.all_to_all(both, "slab", split_axis=2, concat_axis=1, tiled=True),
        precision=lax.Precision.HIGHEST,
    )
    return (smoothed[0][None], smoothed[1][None])


def solution(mesh):
    placed = (
        P("tm", None, "slab", None, None),
        P("tm", "slab", None, None),
        P("slab", None, None),
        P("tm", None, "slab", None, None),
        P(),
        P(),
    )
    return jax.shard_map(
        body,
        mesh=mesh,
        in_specs=placed,
        out_specs=(P("tm", None, "slab"), P("tm", None, "slab")),
        check_vma=False,
    )
```

profile of v0, /device:TPU:0, one launch (start us, length us, event | category | flops | bytes accessed | tf_op | source)
XLA Modules:
  0.0 116.6 jit_solution(5801079610533126494)
XLA Ops:
  0.6 3.0 %collective-permute-start = (f32[16,8,16,128]{3,2,1,0:T(8,128)}, f32[16,8,16,128]{3,2,1,0:T(8,128)S(1)}, u32[]{:S(2)}, u32[]{:S(2)}) collective-permute-start(f32[16,8,16,128]{3,2,1,0:T(8,128)} %bitcast.28), channel_id=1, source_target_pairs={{0,16},{8,24},{16,0},{24,8},{1,17},{9,25},{17,1},{25,9},{2,18},{10... | collective-permute-start | bytes 3145736 | tf_op jit(solution)/shard_map/ppermute | solution.py:29
  4.4 0.8 broadcast_subtract_fusion
  5.3 22.5 %collective-permute-done = f32[16,8,16,128]{3,2,1,0:T(8,128)S(1)} collective-permute-done((f32[16,8,16,128]{3,2,1,0:T(8,128)}, f32[16,8,16,128]{3,2,1,0:T(8,128)S(1)}, u32[]{:S(2)}, u32[]{:S(2)}) %collective-permute-start) | collective-permute-done | bytes 1048608 | tf_op jit(solution)/shard_map/ppermute | solution.py:29
  27.8 1.3 %collective-permute-start.1 = (f32[16,1,16,128]{3,2,1,0:T(8,128)S(1)}, f32[16,1,16,128]{3,2,1,0:T(8,128)S(1)}, u32[]{:S(2)}, u32[]{:S(2)}) collective-permute-start(f32[16,1,16,128]{3,2,1,0:T(8,128)S(1)} %get-tuple-element.27), channel_id=1, source_target_pairs={{1,0},{2,1},{3,2},{4,3},{5,4},{6,5},{7,6},{9,8},{10,9},{11,10},{12... | collective-permute-start | bytes 393224 | tf_op jit(solution)/shard_map/ppermute | solution.py:21
  29.1 3.0 %collective-permute-start.2 = (f32[16,1,16,128]{3,2,1,0:T(8,128)S(1)}, f32[16,1,16,128]{3,2,1,0:T(8,128)S(1)}, u32[]{:S(2)}, u32[]{:S(2)}) collective-permute-start(f32[16,1,16,128]{3,2,1,0:T(8,128)S(1)} %get-tuple-element.28), channel_id=1, source_target_pairs={{0,1},{1,2},{2,3},{3,4},{4,5},{5,6},{6,7},{8,9},{9,10},{10,11},{11... | collective-permute-start | bytes 393224 | tf_op jit(solution)/shard_map/ppermute | solution.py:20
  32.1 0.9 collective-permute-done.2
  33.9 1.3 %collective-permute-start.4 = (f32[16,1,16,128]{3,2,1,0:T(8,128)S(1)}, f32[16,1,16,128]{3,2,1,0:T(8,128)S(1)}, u32[]{:S(2)}, u32[]{:S(2)}) collective-permute-start(f32[16,1,16,128]{3,2,1,0:T(8,128)S(1)} %get-tuple-element.25), channel_id=1, source_target_pairs={{1,0},{2,1},{3,2},{4,3},{5,4},{6,5},{7,6},{9,8},{10,9},{11,10},{12... | collective-permute-start | bytes 393224 | tf_op jit(solution)/shard_map/ppermute | solution.py:21
  35.2 4.9 %collective-permute-start.5 = (f32[16,1,16,128]{3,2,1,0:T(8,128)S(1)}, f32[16,1,16,128]{3,2,1,0:T(8,128)S(1)}, u32[]{:S(2)}, u32[]{:S(2)}) collective-permute-start(f32[16,1,16,128]{3,2,1,0:T(8,128)S(1)} %get-tuple-element.26), channel_id=1, source_target_pairs={{0,1},{1,2},{2,3},{3,4},{4,5},{5,6},{6,7},{8,9},{9,10},{10,11},{11... | collective-permute-start | bytes 393224 | tf_op jit(solution)/shard_map/ppermute | solution.py:20
  40.1 1.0 collective-permute-done.5
  41.9 1.4 %collective-permute-start.6 = (f32[16,1,16,128]{3,2,1,0:T(8,128)S(1)}, f32[16,1,16,128]{3,2,1,0:T(8,128)S(1)}, u32[]{:S(2)}, u32[]{:S(2)}) collective-permute-start(f32[16,1,16,128]{3,2,1,0:T(8,128)S(1)} %get-tuple-element.23), channel_id=1, source_target_pairs={{1,0},{2,1},{3,2},{4,3},{5,4},{6,5},{7,6},{9,8},{10,9},{11,10},{12... | collective-permute-start | bytes 393224 | tf_op jit(solution)/shard_map/ppermute | solution.py:21
  43.3 5.9 %collective-permute-start.7 = (f32[16,1,16,128]{3,2,1,0:T(8,128)S(1)}, f32[16,1,16,128]{3,2,1,0:T(8,128)S(1)}, u32[]{:S(2)}, u32[]{:S(2)}) collective-permute-start(f32[16,1,16,128]{3,2,1,0:T(8,128)S(1)} %get-tuple-element.24), channel_id=1, source_target_pairs={{0,1},{1,2},{2,3},{3,4},{4,5},{5,6},{6,7},{8,9},{9,10},{10,11},{11... | collective-permute-start | bytes 393224 | tf_op jit(solution)/shard_map/ppermute | solution.py:20
  49.3 1.0 collective-permute-done.7
  51.1 1.3 %collective-permute-start.8 = (f32[16,1,16,128]{3,2,1,0:T(8,128)S(1)}, f32[16,1,16,128]{3,2,1,0:T(8,128)S(1)}, u32[]{:S(2)}, u32[]{:S(2)}) collective-permute-start(f32[16,1,16,128]{3,2,1,0:T(8,128)S(1)} %get-tuple-element.21), channel_id=1, source_target_pairs={{1,0},{2,1},{3,2},{4,3},{5,4},{6,5},{7,6},{9,8},{10,9},{11,10},{12... | collective-permute-start | bytes 393224 | tf_op jit(solution)/shard_map/ppermute | solution.py:21
  52.4 5.9 %collective-permute-start.9 = (f32[16,1,16,128]{3,2,1,0:T(8,128)S(1)}, f32[16,1,16,128]{3,2,1,0:T(8,128)S(1)}, u32[]{:S(2)}, u32[]{:S(2)}) collective-permute-start(f32[16,1,16,128]{3,2,1,0:T(8,128)S(1)} %get-tuple-element.22), channel_id=1, source_target_pairs={{0,1},{1,2},{2,3},{3,4},{4,5},{5,6},{6,7},{8,9},{9,10},{10,11},{11... | collective-permute-start | bytes 393224 | tf_op jit(solution)/shard_map/ppermute | solution.py:20
  58.4 1.0 collective-permute-done.9
  60.2 1.3 %collective-permute-start.10 = (f32[16,1,16,128]{3,2,1,0:T(8,128)S(1)}, f32[16,1,16,128]{3,2,1,0:T(8,128)S(1)}, u32[]{:S(2)}, u32[]{:S(2)}) collective-permute-start(f32[16,1,16,128]{3,2,1,0:T(8,128)S(1)} %get-tuple-element.19), channel_id=1, source_target_pairs={{1,0},{2,1},{3,2},{4,3},{5,4},{6,5},{7,6},{9,8},{10,9},{11,10},{12... | collective-permute-start | bytes 393224 | tf_op jit(solution)/shard_map/ppermute | solution.py:21
  61.5 5.9 %collective-permute-start.11 = (f32[16,1,16,128]{3,2,1,0:T(8,128)S(1)}, f32[16,1,16,128]{3,2,1,0:T(8,128)S(1)}, u32[]{:S(2)}, u32[]{:S(2)}) collective-permute-start(f32[16,1,16,128]{3,2,1,0:T(8,128)S(1)} %get-tuple-element.20), channel_id=1, source_target_pairs={{0,1},{1,2},{2,3},{3,4},{4,5},{5,6},{6,7},{8,9},{9,10},{10,11},{11... | collective-permute-start | bytes 393224 | tf_op jit(solution)/shard_map/ppermute | solution.py:20
  67.4 1.0 collective-permute-done.11
  68.4 1.8 %multiply_reduce_fusion.6 = (f32[8,16,128]{2,1,0:T(8,128)S(1)}, f32[8,16,128]{2,1,0:T(8,128)S(1)}, f32[16,8,16,128]{3,2,1,0:T(8,128)S(1)}) fusion(f32[16]{0:T(128)S(1)} %get-tuple-element.31, f32[16,8,16,128]{3,2,1,0:T(8,128)S(1)} %get-tuple-element.10, f32[16,1,16,128]{3,2,1,0:T(8,128)S(1)} %collective-permute-done.11, ...), kind=kLoop, calls=%fused_computation.110 | loop fusion | flops 7307264 | bytes 3932288 | tf_op jit(solution)/shard_map/reduce_sum | solution.py:82
  70.2 1.3 %collective-permute-start.12 = (f32[16,1,16,128]{3,2,1,0:T(8,128)S(1)}, f32[16,1,16,128]{3,2,1,0:T(8,128)S(1)}, u32[]{:S(2)}, u32[]{:S(2)}) collective-permute-start(f32[16,1,16,128]{3,2,1,0:T(8,128)S(1)} %get-tuple-element.17), channel_id=1, source_target_pairs={{1,0},{2,1},{3,2},{4,3},{5,4},{6,5},{7,6},{9,8},{10,9},{11,10},{12... | collective-permute-start | bytes 393224 | tf_op jit(solution)/shard_map/ppermute | solution.py:21
  71.5 5.9 %collective-permute-start.13 = (f32[16,1,16,128]{3,2,1,0:T(8,128)S(1)}, f32[16,1,16,128]{3,2,1,0:T(8,128)S(1)}, u32[]{:S(2)}, u32[]{:S(2)}) collective-permute-start(f32[16,1,16,128]{3,2,1,0:T(8,128)S(1)} %get-tuple-element.18), channel_id=1, source_target_pairs={{0,1},{1,2},{2,3},{3,4},{4,5},{5,6},{6,7},{8,9},{9,10},{10,11},{11... | collective-permute-start | bytes 393224 | tf_op jit(solution)/shard_map/ppermute | solution.py:20
  77.5 1.0 collective-permute-done.13
  78.4 1.8 %multiply_reduce_fusion.5 = (f32[8,16,128]{2,1,0:T(8,128)S(1)}, f32[8,16,128]{2,1,0:T(8,128)S(1)}, f32[16,8,16,128]{3,2,1,0:T(8,128)S(1)}) fusion(f32[16]{0:T(128)S(1)} %get-tuple-element.32, f32[16,8,16,128]{3,2,1,0:T(8,128)S(1)} %get-tuple-element.11, f32[16,1,16,128]{3,2,1,0:T(8,128)S(1)} %collective-permute-done.13, ...), kind=kLoop, calls=%fused_computation.109 | loop fusion | flops 7307264 | bytes 3932288 | tf_op jit(solution)/shard_map/reduce_sum | solution.py:82
  80.2 1.3 %collective-permute-start.14 = (f32[16,1,16,128]{3,2,1,0:T(8,128)S(1)}, f32[16,1,16,128]{3,2,1,0:T(8,128)S(1)}, u32[]{:S(2)}, u32[]{:S(2)}) collective-permute-start(f32[16,1,16,128]{3,2,1,0:T(8,128)S(1)} %get-tuple-element.15), channel_id=1, source_target_pairs={{1,0},{2,1},{3,2},{4,3},{5,4},{6,5},{7,6},{9,8},{10,9},{11,10},{12... | collective-permute-start | bytes 393224 | tf_op jit(solution)/shard_map/ppermute | solution.py:21
  81.5 5.9 %collective-permute-start.15 = (f32[16,1,16,128]{3,2,1,0:T(8,128)S(1)}, f32[16,1,16,128]{3,2,1,0:T(8,128)S(1)}, u32[]{:S(2)}, u32[]{:S(2)}) collective-permute-start(f32[16,1,16,128]{3,2,1,0:T(8,128)S(1)} %get-tuple-element.16), channel_id=1, source_target_pairs={{0,1},{1,2},{2,3},{3,4},{4,5},{5,6},{6,7},{8,9},{9,10},{10,11},{11... | collective-permute-start | bytes 393224 | tf_op jit(solution)/shard_map/ppermute | solution.py:20
  87.5 1.0 collective-permute-done.15
  89.4 1.0 copy.12
  90.4 4.0 %reshape.150 = f32[8,1,4096]{2,1,0:T(1,128)} reshape(f32[2048,2,8]{2,1,0:T(2,128)S(1)} %bitcast.26) | data formatting | bytes 262144
  94.4 9.0 %all-to-all-start = ((f32[8,1,4096]{2,1,0:T(1,128)}), f32[8,1,4096]{2,1,0:T(1,128)S(1)}, u32[]{:S(2)}, u32[]{:S(2)}) async-start(f32[8,1,4096]{2,1,0:T(1,128)} %reshape.150), calls=%async_computation | async-start | bytes 262144 | tf_op jit(solution)/shard_map/all_to_all | solution.py:92
  103.6 6.6 %all-to-all-done = f32[8,1,4096]{2,1,0:T(1,128)S(1)} async-done(((f32[8,1,4096]{2,1,0:T(1,128)}), f32[8,1,4096]{2,1,0:T(1,128)S(1)}, u32[]{:S(2)}, u32[]{:S(2)}) %all-to-all-start) | async-done | bytes 131104 | tf_op jit(solution)/shard_map/all_to_all | solution.py:92
  110.7 1.0 reduce
  111.7 3.2 %reshape.151 = f32[2048,2,8]{2,1,0:T(2,128)S(1)} reshape(f32[8,4096]{1,0:T(8,128)S(1)} %reduce) | data formatting | bytes 262144
  (37 shorter events, 7.5 us)
Async XLA Ops:
  0.6 27.1 %collective-permute-start = (f32[16,8,16,128]{3,2,1,0:T(8,128)}, f32[16,8,16,128]{3,2,1,0:T(8,128)S(1)}, u32[]{:S(2)}, u32[]{:S(2)}) collective-permute-start(f32[16,8,16,128]{3,2,1,0:T(8,128)} %bitcast.28), channel_id=1, source_target_pairs={{0,16},{8,24},{16,0},{24,8},{1,17},{9,25},{17,1},{25,9},{2,18},{10... | collective-permute-start | bytes 3145736 | tf_op jit(solution)/shard_map/ppermute | solution.py:29
  3.7 28.5 %collective-permute-start.3 = (f32[8,16,128]{2,1,0:T(8,128)}, f32[8,16,128]{2,1,0:T(8,128)S(1)}, u32[]{:S(2)}, u32[]{:S(2)}) collective-permute-start(f32[8,16,128]{2,1,0:T(8,128)} %bitcast.29), channel_id=1, source_target_pairs={{0,16},{8,24},{16,0},{24,8},{1,17},{9,25},{17,1},{25,9},{2,18},{10... | collective-permute-start | bytes 196616 | tf_op jit(solution)/shard_map/ppermute | solution.py:29
  27.8 4.4 %collective-permute-start.1 = (f32[16,1,16,128]{3,2,1,0:T(8,128)S(1)}, f32[16,1,16,128]{3,2,1,0:T(8,128)S(1)}, u32[]{:S(2)}, u32[]{:S(2)}) collective-permute-start(f32[16,1,16,128]{3,2,1,0:T(8,128)S(1)} %get-tuple-element.27), channel_id=1, source_target_pairs={{1,0},{2,1},{3,2},{4,3},{5,4},{6,5},{7,6},{9,8},{10,9},{11,10},{12... | collective-permute-start | bytes 393224 | tf_op jit(solution)/shard_map/ppermute | solution.py:21
  29.1 4.0 %collective-permute-start.2 = (f32[16,1,16,128]{3,2,1,0:T(8,128)S(1)}, f32[16,1,16,128]{3,2,1,0:T(8,128)S(1)}, u32[]{:S(2)}, u32[]{:S(2)}) collective-permute-start(f32[16,1,16,128]{3,2,1,0:T(8,128)S(1)} %get-tuple-element.28), channel_id=1, source_target_pairs={{0,1},{1,2},{2,3},{3,4},{4,5},{5,6},{6,7},{8,9},{9,10},{10,11},{11... | collective-permute-start | bytes 393224 | tf_op jit(solution)/shard_map/ppermute | solution.py:20
  33.9 6.2 %collective-permute-start.4 = (f32[16,1,16,128]{3,2,1,0:T(8,128)S(1)}, f32[16,1,16,128]{3,2,1,0:T(8,128)S(1)}, u32[]{:S(2)}, u32[]{:S(2)}) collective-permute-start(f32[16,1,16,128]{3,2,1,0:T(8,128)S(1)} %get-tuple-element.25), channel_id=1, source_target_pairs={{1,0},{2,1},{3,2},{4,3},{5,4},{6,5},{7,6},{9,8},{10,9},{11,10},{12... | collective-permute-start | bytes 393224 | tf_op jit(solution)/shard_map/ppermute | solution.py:21
  35.2 5.9 %collective-permute-start.5 = (f32[16,1,16,128]{3,2,1,0:T(8,128)S(1)}, f32[16,1,16,128]{3,2,1,0:T(8,128)S(1)}, u32[]{:S(2)}, u32[]{:S(2)}) collective-permute-start(f32[16,1,16,128]{3,2,1,0:T(8,128)S(1)} %get-tuple-element.26), channel_id=1, source_target_pairs={{0,1},{1,2},{2,3},{3,4},{4,5},{5,6},{6,7},{8,9},{9,10},{10,11},{11... | collective-permute-start | bytes 393224 | tf_op jit(solution)/shard_map/ppermute | solution.py:20
  41.9 17.5 %copy-start = (f32[1,16,8,16,128]{4,3,2,1,0:T(8,128)S(1)}, f32[1,16,8,16,128]{4,3,2,1,0:T(8,128)}, u32[]{:S(2)}) copy-start(f32[1,16,8,16,128]{4,3,2,1,0:T(8,128)} %param.9) | copy-start | bytes 3145732
  41.9 7.4 %collective-permute-start.6 = (f32[16,1,16,128]{3,2,1,0:T(8,128)S(1)}, f32[16,1,16,128]{3,2,1,0:T(8,128)S(1)}, u32[]{:S(2)}, u32[]{:S(2)}) collective-permute-start(f32[16,1,16,128]{3,2,1,0:T(8,128)S(1)} %get-tuple-element.23), channel_id=1, source_target_pairs={{1,0},{2,1},{3,2},{4,3},{5,4},{6,5},{7,6},{9,8},{10,9},{11,10},{12... | collective-permute-start | bytes 393224 | tf_op jit(solution)/shard_map/ppermute | solution.py:21
  43.3 6.9 %collective-permute-start.7 = (f32[16,1,16,128]{3,2,1,0:T(8,128)S(1)}, f32[16,1,16,128]{3,2,1,0:T(8,128)S(1)}, u32[]{:S(2)}, u32[]{:S(2)}) collective-permute-start(f32[16,1,16,128]{3,2,1,0:T(8,128)S(1)} %get-tuple-element.24), channel_id=1, source_target_pairs={{0,1},{1,2},{2,3},{3,4},{4,5},{5,6},{6,7},{8,9},{9,10},{10,11},{11... | collective-permute-start | bytes 393224 | tf_op jit(solution)/shard_map/ppermute | solution.py:20
  51.1 7.3 %collective-permute-start.8 = (f32[16,1,16,128]{3,2,1,0:T(8,128)S(1)}, f32[16,1,16,128]{3,2,1,0:T(8,128)S(1)}, u32[]{:S(2)}, u32[]{:S(2)}) collective-permute-start(f32[16,1,16,128]{3,2,1,0:T(8,128)S(1)} %get-tuple-element.21), channel_id=1, source_target_pairs={{1,0},{2,1},{3,2},{4,3},{5,4},{6,5},{7,6},{9,8},{10,9},{11,10},{12... | collective-permute-start | bytes 393224 | tf_op jit(solution)/shard_map/ppermute | solution.py:21
  52.4 6.9 %collective-permute-start.9 = (f32[16,1,16,128]{3,2,1,0:T(8,128)S(1)}, f32[16,1,16,128]{3,2,1,0:T(8,128)S(1)}, u32[]{:S(2)}, u32[]{:S(2)}) collective-permute-start(f32[16,1,16,128]{3,2,1,0:T(8,128)S(1)} %get-tuple-element.22), channel_id=1, source_target_pairs={{0,1},{1,2},{2,3},{3,4},{4,5},{5,6},{6,7},{8,9},{9,10},{10,11},{11... | collective-permute-start | bytes 393224 | tf_op jit(solution)/shard_map/ppermute | solution.py:20
  60.2 7.3 %collective-permute-start.10 = (f32[16,1,16,128]{3,2,1,0:T(8,128)S(1)}, f32[16,1,16,128]{3,2,1,0:T(8,128)S(1)}, u32[]{:S(2)}, u32[]{:S(2)}) collective-permute-start(f32[16,1,16,128]{3,2,1,0:T(8,128)S(1)} %get-tuple-element.19), channel_id=1, source_target_pairs={{1,0},{2,1},{3,2},{4,3},{5,4},{6,5},{7,6},{9,8},{10,9},{11,10},{12... | collective-permute-start | bytes 393224 | tf_op jit(solution)/shard_map/ppermute | solution.py:21
  61.5 6.9 %collective-permute-start.11 = (f32[16,1,16,128]{3,2,1,0:T(8,128)S(1)}, f32[16,1,16,128]{3,2,1,0:T(8,128)S(1)}, u32[]{:S(2)}, u32[]{:S(2)}) collective-permute-start(f32[16,1,16,128]{3,2,1,0:T(8,128)S(1)} %get-tuple-element.20), channel_id=1, source_target_pairs={{0,1},{1,2},{2,3},{3,4},{4,5},{5,6},{6,7},{8,9},{9,10},{10,11},{11... | collective-permute-start | bytes 393224 | tf_op jit(solution)/shard_map/ppermute | solution.py:20
  70.2 7.3 %collective-permute-start.12 = (f32[16,1,16,128]{3,2,1,0:T(8,128)S(1)}, f32[16,1,16,128]{3,2,1,0:T(8,128)S(1)}, u32[]{:S(2)}, u32[]{:S(2)}) collective-permute-start(f32[16,1,16,128]{3,2,1,0:T(8,128)S(1)} %get-tuple-element.17), channel_id=1, source_target_pairs={{1,0},{2,1},{3,2},{4,3},{5,4},{6,5},{7,6},{9,8},{10,9},{11,10},{12... | collective-permute-start | bytes 393224 | tf_op jit(solution)/shard_map/ppermute | solution.py:21
  71.5 6.9 %collective-permute-start.13 = (f32[16,1,16,128]{3,2,1,0:T(8,128)S(1)}, f32[16,1,16,128]{3,2,1,0:T(8,128)S(1)}, u32[]{:S(2)}, u32[]{:S(2)}) collective-permute-start(f32[16,1,16,128]{3,2,1,0:T(8,128)S(1)} %get-tuple-element.18), channel_id=1, source_target_pairs={{0,1},{1,2},{2,3},{3,4},{4,5},{5,6},{6,7},{8,9},{9,10},{10,11},{11... | collective-permute-start | bytes 393224 | tf_op jit(solution)/shard_map/ppermute | solution.py:20
  80.2 7.3 %collective-permute-start.14 = (f32[16,1,16,128]{3,2,1,0:T(8,128)S(1)}, f32[16,1,16,128]{3,2,1,0:T(8,128)S(1)}, u32[]{:S(2)}, u32[]{:S(2)}) collective-permute-start(f32[16,1,16,128]{3,2,1,0:T(8,128)S(1)} %get-tuple-element.15), channel_id=1, source_target_pairs={{1,0},{2,1},{3,2},{4,3},{5,4},{6,5},{7,6},{9,8},{10,9},{11,10},{12... | collective-permute-start | bytes 393224 | tf_op jit(solution)/shard_map/ppermute | solution.py:21
  81.5 6.9 %collective-permute-start.15 = (f32[16,1,16,128]{3,2,1,0:T(8,128)S(1)}, f32[16,1,16,128]{3,2,1,0:T(8,128)S(1)}, u32[]{:S(2)}, u32[]{:S(2)}) collective-permute-start(f32[16,1,16,128]{3,2,1,0:T(8,128)S(1)} %get-tuple-element.16), channel_id=1, source_target_pairs={{0,1},{1,2},{2,3},{3,4},{4,5},{5,6},{6,7},{8,9},{9,10},{10,11},{11... | collective-permute-start | bytes 393224 | tf_op jit(solution)/shard_map/ppermute | solution.py:20
  89.3 14.1 %copy-start.1 = (f32[31]{0:T(128)S(1)}, f32[31]{0:T(128)}, u32[]{:S(2)}) copy-start(f32[31]{0:T(128)} %param.11) | copy-start | bytes 376
  94.4 15.8 %all-to-all-start = ((f32[8,1,4096]{2,1,0:T(1,128)}), f32[8,1,4096]{2,1,0:T(1,128)S(1)}, u32[]{:S(2)}, u32[]{:S(2)}) async-start(f32[8,1,4096]{2,1,0:T(1,128)} %reshape.150), calls=%async_computation | async-start | bytes 262144 | tf_op jit(solution)/shard_map/all_to_all | solution.py:92
where the time goes:
time: 117 us
  starting transfers between devices  59 us (50%)
  waiting for transfers between devices  35.7 us (31%)
  other arithmetic  10.3 us (9%)
  local copies, waits for them, and re-layouts  10.3 us (9%)
    ppermute x7, starting transfers between devices, extended(): before = lax.ppermute(last, axis, up)  37.7 us
    ppermute x2, waiting for transfers between devices, shifted(): return lax.ppermute(value, axis, pairs)  22.5 us
    ppermute x7, starting transfers between devices, extended(): after = lax.ppermute(first, axis, down)  9.18 us
    all_to_all x1, starting transfers between devices, body(): lax.all_to_all(both, 'slab', split_axis=2, concat_axis=1, tiled=True)  9.04 us
    unnamed x6, local copies, waits for them, and re-layouts  7.16 us
    ppermute x7, waiting for transfers between devices, extended(): before = lax.ppermute(last, axis, up)  6.63 us
    all_to_all x1, waiting for transfers between devices, body(): lax.all_to_all(both, 'slab', split_axis=2, concat_axis=1, tiled=True)  6.56 us
    reduce_sum x4, other arithmetic, body(): jnp.sum(chosen[:, None, None, None] * adjoint, axis=0)  5.16 us
  transfers between devices with their start and end apart: 17, of which 9 were waited for; matrix products, arithmetic and copies ran while one was open for 2% of the time, Pallas kernels for 0%

commit v1 on v0

v1 whole, which is shorter than its diff:
```python
import functools

import jax
import jax.numpy as jnp
from jax import lax
from jax.experimental import pallas as pl
from jax.experimental.pallas import tpu as pltpu
from jax.sharding import PartitionSpec as P

STEPS = 4
LANES = 128
vertical_rate = 0.2
lateral_rate = 0.1

MESH = pl.DeviceIdType.MESH
WIDE = STEPS
SIDE = STEPS - 1


def operator(v, centre, edges):
    left, right, front, back = edges
    middle = v[1:-1]
    count, ny, nx = middle.shape
    flat = middle.reshape(count * ny, nx)
    west = pltpu.roll(flat, 1, axis=1).reshape(middle.shape)
    east = pltpu.roll(flat, nx - 1, axis=1).reshape(middle.shape)
    south = pltpu.roll(flat, 1, axis=0).reshape(middle.shape)
    north = pltpu.roll(flat, count * ny - 1, axis=0).reshape(middle.shape)
    lateral = west * left + east * right + south * front + north * back
    return middle * centre + vertical_rate * (v[2:] + v[:-2]) + lateral


def inside(v, width, low, high):
    return jnp.concatenate([v[:width] * low, v[width:-width], v[-width:] * high], axis=0)


def kernel(
    groups,
    slabs,
    release_ref,
    taps_ref,
    initial_ref,
    source_ref,
    decay_ref,
    observed_ref,
    source_out,
    decay_out,
    start,
    centre,
    field,
    states,
    final,
    target,
    adjoint,
    total,
    turned,
    columns,
    matrix,
    local_sem,
    side_send,
    side_recv,
    obs_send,
    obs_recv,
    halo_send,
    halo_recv,
    turn_send,
    turn_recv,
):
    tm = lax.axis_index("tm")
    slab = lax.axis_index("slab")
    partner = lax.rem(tm + groups // 2, groups)
    channels, _, ny, nx = start.shape
    local = decay_ref.shape[0]
    depth = matrix.shape[0]
    rows = columns.shape[1]
    width = source_out.shape[2]
    has_low = slab > 0
    has_high = slab < slabs - 1

    def local_copies():
        return (
            pltpu.make_async_copy(initial_ref.at[0], start.at[:, pl.ds(WIDE, local)], local_sem.at[0]),
            pltpu.make_async_copy(source_ref.at[0], field.at[pl.ds(SIDE, local)], local_sem.at[1]),
            pltpu.make_async_copy(decay_ref, centre.at[pl.ds(SIDE, local)], local_sem.at[2]),
        )

    def remote(src, dst, send, recv, to_tm, to_slab):
        return pltpu.make_async_remote_copy(
            src_ref=src,
            dst_ref=dst,
            send_sem=send,
            recv_sem=recv,
            device_id=(to_tm, to_slab),
            device_id_type=MESH,
        )

    def to_high():
        other = slab + 1
        return (
            remote(decay_ref.at[pl.ds(local - SIDE, SIDE)], centre.at[pl.ds(0, SIDE)], side_send.at[0], side_recv.at[0], tm, other),
            remote(source_ref.at[0, pl.ds(local - SIDE, SIDE)], field.at[pl.ds(0, SIDE)], side_send.at[1], side_recv.at[1], tm, other),
            remote(initial_ref.at[0, :, pl.ds(local - WIDE, WIDE)], start.at[:, pl.ds(0, WIDE)], side_send.at[2], side_recv.at[2], tm, other),
        )

    def to_low():
        other = slab - 1
        return (
            remote(decay_ref.at[pl.ds(0, SIDE)], centre.at[pl.ds(SIDE + local, SIDE)], side_send.at[3], side_recv.at[3], tm, other),
            remote(source_ref.at[0, pl.ds(0, SIDE)], field.at[pl.ds(SIDE + local, SIDE)], side_send.at[4], side_recv.at[4], tm, other),
            remote(initial_ref.at[0, :, pl.ds(0, WIDE)], start.at[:, pl.ds(WIDE + local, WIDE)], side_send.at[5], side_recv.at[5], tm, other),
        )

    def observation(c):
        return remote(observed_ref.at[0, c], target.at[c], obs_send.at[c], obs_recv.at[c], partner, slab)

    def halo_high(c):
        return remote(
            adjoint.at[c, pl.ds(local, SIDE)], adjoint.at[c, pl.ds(0, SIDE)], halo_send.at[0, c], halo_recv.at[0, c], tm, slab + 1
        )

    def halo_low(c):
        return remote(
            adjoint.at[c, pl.ds(SIDE, SIDE)], adjoint.at[c, pl.ds(SIDE + local, SIDE)], halo_send.at[1, c], halo_recv.at[1, c], tm, slab - 1
        )

    def turn(other):
        return remote(
            turned.at[:, pl.ds((other * width) // nx, rows)],
            columns.at[:, :, pl.ds(pl.multiple_of(slab * local, local), local)],
            turn_send.at[other],
            turn_recv.at[slab],
            partner,
            other,
        )

    for copy in local_copies():
        copy.start()

    barrier = pltpu.get_barrier_semaphore()

    @pl.loop(0, slabs)
    def _(other):
        pl.semaphore_signal(barrier, inc=1, device_id=(partner, other), device_id_type=MESH)

    @pl.when(has_low)
    def _():
        pl.semaphore_signal(barrier, inc=1, device_id=(tm, slab - 1), device_id_type=MESH)

    @pl.when(has_high)
    def _():
        pl.semaphore_signal(barrier, inc=1, device_id=(tm, slab + 1), device_id_type=MESH)

    pl.semaphore_wait(barrier, slabs + has_low.astype(jnp.int32) + has_high.astype(jnp.int32))

    observation(0).start()

    @pl.when(has_high)
    def _():
        for copy in to_high():
            copy.start()

    @pl.when(has_low)
    def _():
        for copy in to_low():
            copy.start()

    @pl.loop(1, channels)
    def _(c):
        observation(c).start()

    @pl.when(jnp.logical_not(has_low))
    def _():
        centre[pl.ds(0, SIDE)] = jnp.zeros((SIDE, ny, nx), jnp.float32)
        field[pl.ds(0, SIDE)] = jnp.zeros((SIDE, ny, nx), jnp.float32)
        start[:, pl.ds(0, WIDE)] = jnp.zeros((channels, WIDE, ny, nx), jnp.float32)
        adjoint[:, pl.ds(0, SIDE)] = jnp.zeros((channels, SIDE, ny, nx), jnp.float32)

    @pl.when(jnp.logical_not(has_high))
    def _():
        centre[pl.ds(SIDE + local, SIDE)] = jnp.zeros((SIDE, ny, nx), jnp.float32)
        field[pl.ds(SIDE + local, SIDE)] = jnp.zeros((SIDE, ny, nx), jnp.float32)
        start[:, pl.ds(WIDE + local, WIDE)] = jnp.zeros((channels, WIDE, ny, nx), jnp.float32)
        adjoint[:, pl.ds(SIDE + local, SIDE)] = jnp.zeros((channels, SIDE, ny, nx), jnp.float32)

    low = jnp.where(has_low, 1.0, 0.0).astype(jnp.float32)
    high = jnp.where(has_high, 1.0, 0.0).astype(jnp.float32)

    taps = taps_ref.shape[0]
    offset = (
        lax.broadcasted_iota(jnp.int32, (depth, depth), 1)
        - lax.broadcasted_iota(jnp.int32, (depth, depth), 0)
        + (taps - 1) // 2
    )
    matrix[...] = jnp.zeros_like(matrix)
    for tap in range(taps):
        matrix[...] += jnp.where(offset == tap, taps_ref[tap], 0.0)

    total[...] = jnp.zeros_like(total)

    x_at = lax.broadcasted_iota(jnp.int32, (ny, nx), 1)
    y_at = lax.broadcasted_iota(jnp.int32, (ny, nx), 0)
    edges = tuple(
        jnp.where(place, 0.0, lateral_rate).astype(jnp.float32)
        for place in (x_at == 0, x_at == nx - 1, y_at == 0, y_at == ny - 1)
    )

    for copy in local_copies():
        copy.wait()

    @pl.when(has_low)
    def _():
        for copy in to_high():
            copy.wait_recv()

    @pl.when(has_high)
    def _():
        for copy in to_low():
            copy.wait_recv()

    centre[...] = (1.0 - 2.0 * vertical_rate - 4.0 * lateral_rate) - centre[...]

    @pl.loop(0, channels)
    def _(c):
        when = release_ref[tm, c]
        current = start[c]
        for step in range(STEPS):
            halo = SIDE - step
            chosen = jnp.where(when == step, 1.0, 0.0).astype(jnp.float32)
            part = pl.ds(step, local + 2 * halo)
            current = operator(current, centre[part], edges) + chosen * field[part]
            if halo:
                current = inside(current, halo, low, high)
                states[c, step] = current[halo:-halo]
            else:
                final[c] = current

    def backward(c):
        when = release_ref[tm, c]
        current = adjoint[c]
        decay_sum = total[1]
        source_sum = total[0]
        for step in reversed(range(STEPS)):
            own = current[step : step + local]
            chosen = jnp.where(when == step, 1.0, 0.0).astype(jnp.float32)
            source_sum = source_sum + chosen * own
            past = states[c, step - 1] if step else start[c, pl.ds(WIDE, local)]
            decay_sum = decay_sum - own * past
            if step:
                halo = step - 1
                current = operator(current, centre[pl.ds(SIDE - halo, local + 2 * halo)], edges)
                if halo:
                    current = inside(current, halo, low, high)
        total[0] = source_sum
        total[1] = decay_sum

    def await_halo(c):
        @pl.when(has_low)
        def _():
            halo_high(c).wait_recv()

        @pl.when(has_high)
        def _():
            halo_low(c).wait_recv()

    @pl.loop(0, channels)
    def _(c):
        observation(c).wait_recv()
        adjoint[c, pl.ds(SIDE, local)] = final[c] - target[c]

        @pl.when(has_high)
        def _():
            halo_high(c).start()

        @pl.when(has_low)
        def _():
            halo_low(c).start()

        @pl.when(c > 0)
        def _():
            await_halo(c - 1)
            backward(c - 1)

    await_halo(channels - 1)
    backward(channels - 1)

    for kind in range(2):
        turned[kind] = jnp.swapaxes(total[kind], 0, 1)

    @pl.loop(0, slabs)
    def _(step):
        turn(lax.rem(slab + slabs // 2 + step, slabs)).start()

    @pl.when(has_high)
    def _():
        for copy in to_high():
            copy.wait_send()

    @pl.when(has_low)
    def _():
        for copy in to_low():
            copy.wait_send()

    @pl.loop(0, channels)
    def _(c):
        observation(c).wait_send()

        @pl.when(has_high)
        def _():
            halo_high(c).wait_send()

        @pl.when(has_low)
        def _():
            halo_low(c).wait_send()

    @pl.loop(0, slabs)
    def _(other):
        remote(
            turned.at[:, pl.ds(0, rows)],
            columns.at[:, :, pl.ds(pl.multiple_of(other * local, local), local)],
            turn_send.at[other],
            turn_recv.at[other],
            partner,
            other,
        ).wait_recv()

    for kind, out in enumerate((source_out, decay_out)):
        for row in range(rows):
            smooth = jnp.dot(
                matrix[...], columns[kind, row], precision=lax.Precision.HIGHEST, preferred_element_type=jnp.float32
            )
            if width < nx:
                smooth = pltpu.roll(smooth, lax.rem(nx - lax.rem(slab * width, nx), nx), axis=1)[:, :width]
                out[0] = smooth
            else:
                out[0, :, pl.ds(row * nx, nx)] = smooth

    @pl.loop(0, slabs)
    def _(other):
        turn(other).wait_send()


def solution(mesh):
    groups, slabs = mesh.shape["tm"], mesh.shape["slab"]
    placed = (
        P("tm", None, "slab", None, None),
        P("tm", "slab", None, None),
        P("slab", None, None),
        P("tm", None, "slab", None, None),
        P(),
        P(),
    )

    def body(initial, source, decay_rate, observed, release, smooth_taps):
        _, channels, local, ny, nx = initial.shape
        depth = local * slabs
        width = ny * nx // slabs
        rows = max(1, width // nx)
        assert groups % 2 == 0 and local >= WIDE
        assert width % nx == 0 or nx % width == 0
        f32 = jnp.float32
        anywhere = pl.BlockSpec(memory_space=pl.ANY)
        scalars = pl.BlockSpec(memory_space=pltpu.SMEM)
        out = jax.ShapeDtypeStruct((1, depth, width), f32)
        dma = pltpu.SemaphoreType.DMA
        return pl.pallas_call(
            functools.partial(kernel, groups, slabs),
            out_shape=(out, out),
            in_specs=[scalars, scalars] + [anywhere] * 4,
            out_specs=[pl.BlockSpec(memory_space=pltpu.VMEM)] * 2,
            scratch_shapes=[
                pltpu.VMEM((channels, local + 2 * WIDE, ny, nx), f32),
                pltpu.VMEM((local + 2 * SIDE, ny, nx), f32),
                pltpu.VMEM((local + 2 * SIDE, ny, nx), f32),
                pltpu.VMEM((channels, STEPS - 1, local, ny, nx), f32),
                pltpu.VMEM((channels, local, ny, nx), f32),
                pltpu.VMEM((channels, local, ny, nx), f32),
                pltpu.VMEM((channels, local + 2 * SIDE, ny, nx), f32),
                pltpu.VMEM((2, local, ny, nx), f32),
                pltpu.VMEM((2, ny, local, nx), f32),
                pltpu.VMEM((2, rows, depth, nx), f32),
                pltpu.VMEM((depth, depth), f32),
                dma((3,)),
                dma((6,)),
                dma((6,)),
                dma((channels,)),
                dma((channels,)),
                dma((2, channels)),
                dma((2, channels)),
                dma((slabs,)),
                dma((slabs,)),
            ],
            compiler_params=pltpu.CompilerParams(
                collective_id=0, has_side_effects=True, vmem_limit_bytes=40 * 1024 * 1024
            ),
        )(release, smooth_taps, initial, source, decay_rate, observed)

    return jax.shard_map(
        body,
        mesh=mesh,
        in_specs=placed,
        out_specs=(P("tm", None, "slab"), P("tm", None, "slab")),
        check_vma=False,
    )
```

time: 117 us -> 57.3 us (0.49)
  starting transfers between devices: 59 us -> 0 us
  Pallas kernels: 0 us -> 49.6 us
  waiting for transfers between devices: 35.7 us -> 0 us
  other arithmetic: 10.3 us -> 0 us
  local copies, waits for them, and re-layouts: 10.3 us -> 6.72 us
    ppermute x16 -> x0, starting transfers between devices: 50 us -> none  [the longest x7 37.7 us: extended(): before = lax.ppermute(last, axis, up)]
    pallas_call x0 -> x1, Pallas kernels: none -> 49.6 us  [body(): pl.pallas_call(functools.partial(kernel, groups, slabs), out_shape=(out,...]
    ppermute x16 -> x0, waiting for transfers between devices: 29.1 us -> none  [the longest x2 22.5 us: shifted(): return lax.ppermute(value, axis, pairs)]
    all_to_all x1 -> x0, starting transfers between devices: 9.04 us -> none  [body(): lax.all_to_all(both, 'slab', split_axis=2, concat_axis=1, tiled=True)]
    all_to_all x1 -> x0, waiting for transfers between devices: 6.56 us -> none  [body(): lax.all_to_all(both, 'slab', split_axis=2, concat_axis=1, tiled=True)]
    reduce_sum x5 -> x0, other arithmetic: 5.35 us -> none  [the longest x4 5.16 us: body(): jnp.sum(chosen[:, None, None, None] * adjoint, axis=0)]
    add x4 -> x0, other arithmetic: 2.39 us -> none  [the longest x3 2.38 us: run_forward(): apply_operator(current, decay_rate)]
    all_to_all x2 -> x0, local copies, waits for them, and re-layouts: 1.34 us -> none  [body(): lax.all_to_all(both, 'slab', split_axis=2, concat_axis=1, tiled=True)]
  transfers between devices with their start and end apart: 17 -> 0, of which waited for: 9 -> 0; matrix products, arithmetic and copies ran while one was open for 2% -> 0% of each run, Pallas kernels for 0% -> 0%
where the time goes in v1:
time: 57.3 us; the launch traced here: 56.9 us
  Pallas kernels  49.6 us (87%)
  local copies, waits for them, and re-layouts  6.72 us (12%)
  between operations  0.65 us (1%)
    pallas_call x1, Pallas kernels, body(): pl.pallas_call(functools.partial(kernel, groups, slabs), out_shape=(out,...  49.6 us
    unnamed x14, local copies, waits for them, and re-layouts  6.72 us

profile of v1, /device:TPU:0, one launch (start us, length us, event | category | flops | bytes accessed | tf_op | source)
XLA Modules:
  0.0 56.9 jit_solution(3656732037315730647)
XLA Ops:
  0.6 0.0 copy-start
  0.6 1.2 %copy-done = f32[1,16,8,16,128]{4,3,2,1,0:T(8,128)S(1)} copy-done((f32[1,16,8,16,128]{4,3,2,1,0:T(8,128)S(1)}, f32[1,16,8,16,128]{4,3,2,1,0:T(8,128)}, u32[]{:S(2)}) %copy-start) | copy-done | bytes 1048600
  1.9 0.0 copy-start.1
  1.9 1.2 %copy-done.1 = f32[1,16,8,16,128]{4,3,2,1,0:T(8,128)S(1)} copy-done((f32[1,16,8,16,128]{4,3,2,1,0:T(8,128)S(1)}, f32[1,16,8,16,128]{4,3,2,1,0:T(8,128)}, u32[]{:S(2)}) %copy-start.1) | copy-done | bytes 1048600
  3.1 0.0 copy-start.2
  3.1 0.8 %copy-done.2 = f32[1,8,16,128]{3,2,1,0:T(8,128)S(1)} copy-done((f32[1,8,16,128]{3,2,1,0:T(8,128)S(1)}, f32[1,8,16,128]{3,2,1,0:T(8,128)}, u32[]{:S(2)}) %copy-start.2) | copy-done | bytes 65560
  3.9 0.0 copy-start.3
  3.9 0.8 %copy-done.3 = f32[8,16,128]{2,1,0:T(8,128)S(1)} copy-done((f32[8,16,128]{2,1,0:T(8,128)S(1)}, f32[8,16,128]{2,1,0:T(8,128)}, u32[]{:S(2)}) %copy-start.3) | copy-done | bytes 65560
  4.8 0.0 copy-start.4
  4.8 0.7 %copy-done.4 = s32[4,16]{1,0:T(4,128)S(1)} copy-done((s32[4,16]{1,0:T(4,128)S(1)}, s32[4,16]{1,0:T(4,128)}, u32[]{:S(2)}) %copy-start.4) | copy-done | bytes 280
  5.4 0.0 copy-start.5
  5.4 0.7 %copy-done.5 = f32[31]{0:T(128)S(1)} copy-done((f32[31]{0:T(128)S(1)}, f32[31]{0:T(128)}, u32[]{:S(2)}) %copy-start.5) | copy-done | bytes 148
  6.1 49.6 %shard_map.77 = (f32[1,64,256]{2,1,0:T(8,128)S(1)}, f32[1,64,256]{2,1,0:T(8,128)S(1)}) custom-call(s32[4,16]{1,0:T(4,128)S(1)} %copy-done.4, f32[31]{0:T(128)S(1)} %copy-done.5, f32[1,16,8,16,128]{4,3,2,1,0:T(8,128)S(1)} %copy-done, f32[1,8,16,128]{3,2,1,0:T(8,128)S(1)} %copy-done.2, f32[8,16,128]{2,1,0:T(8,128)S(1)} %copy-done.3, ...), custom_call_target="tpu_custom_call" | custom-call | tf_op jit(solution)/shard_map/pallas_call | solution.py:365
  55.7 0.6 %copy.10 = f32[1,64,256]{2,1,0:T(8,128)} copy(f32[1,64,256]{2,1,0:T(8,128)S(1)} %get-tuple-element.4) | data formatting | bytes 131072
  56.3 0.6 %copy.11 = f32[1,64,256]{2,1,0:T(8,128)} copy(f32[1,64,256]{2,1,0:T(8,128)S(1)} %get-tuple-element.5) | data formatting | bytes 131072
Async XLA Ops:
  0.6 1.2 %copy-start = (f32[1,16,8,16,128]{4,3,2,1,0:T(8,128)S(1)}, f32[1,16,8,16,128]{4,3,2,1,0:T(8,128)}, u32[]{:S(2)}) copy-start(f32[1,16,8,16,128]{4,3,2,1,0:T(8,128)} %initial_ref.1) | copy-start | bytes 3145732
  1.9 1.2 %copy-start.1 = (f32[1,16,8,16,128]{4,3,2,1,0:T(8,128)S(1)}, f32[1,16,8,16,128]{4,3,2,1,0:T(8,128)}, u32[]{:S(2)}) copy-start(f32[1,16,8,16,128]{4,3,2,1,0:T(8,128)} %observed_ref.1) | copy-start | bytes 3145732
  3.1 0.8 %copy-start.2 = (f32[1,8,16,128]{3,2,1,0:T(8,128)S(1)}, f32[1,8,16,128]{3,2,1,0:T(8,128)}, u32[]{:S(2)}) copy-start(f32[1,8,16,128]{3,2,1,0:T(8,128)} %source_ref.1) | copy-start | bytes 196612
  3.9 0.8 %copy-start.3 = (f32[8,16,128]{2,1,0:T(8,128)S(1)}, f32[8,16,128]{2,1,0:T(8,128)}, u32[]{:S(2)}) copy-start(f32[8,16,128]{2,1,0:T(8,128)} %decay_ref.1) | copy-start | bytes 196612
  4.8 0.7 %copy-start.4 = (s32[4,16]{1,0:T(4,128)S(1)}, s32[4,16]{1,0:T(4,128)}, u32[]{:S(2)}) copy-start(s32[4,16]{1,0:T(4,128)} %release_ref.1) | copy-start | bytes 772
  5.4 0.7 %copy-start.5 = (f32[31]{0:T(128)S(1)}, f32[31]{0:T(128)}, u32[]{:S(2)}) copy-start(f32[31]{0:T(128)} %taps_ref.1) | copy-start | bytes 376

commit v2 on v1

--- a/solution.py
+++ b/solution.py
@@ -14,6 +14,8 @@
 
 MESH = pl.DeviceIdType.MESH
 WIDE = STEPS
+GROUP = 2
+LAG = 1
 SIDE = STEPS - 1
 
 
@@ -37,28 +39,29 @@
 def kernel(
     groups,
     slabs,
-    release_ref,
-    taps_ref,
+    release_in,
+    taps_in,
     initial_ref,
     source_ref,
     decay_ref,
     observed_ref,
-    source_out,
-    decay_out,
+    columns,
+    matrix,
     start,
     centre,
     field,
     states,
-    final,
     target,
     adjoint,
     total,
     turned,
-    columns,
-    matrix,
+    release_ref,
+    taps_ref,
     local_sem,
     side_send,
     side_recv,
+    start_send,
+    start_recv,
     obs_send,
     obs_recv,
     halo_send,
@@ -71,9 +74,10 @@
     partner = lax.rem(tm + groups // 2, groups)
     channels, _, ny, nx = start.shape
     local = decay_ref.shape[0]
+    parcels = channels // GROUP
     depth = matrix.shape[0]
     rows = columns.shape[1]
-    width = source_out.shape[2]
+    width = ny * nx // slabs
     has_low = slab > 0
     has_high = slab < slabs - 1
 
@@ -82,6 +86,8 @@
             pltpu.make_async_copy(initial_ref.at[0], start.at[:, pl.ds(WIDE, local)], local_sem.at[0]),
             pltpu.make_async_copy(source_ref.at[0], field.at[pl.ds(SIDE, local)], local_sem.at[1]),
             pltpu.make_async_copy(decay_ref, centre.at[pl.ds(SIDE, local)], local_sem.at[2]),
+            pltpu.make_async_copy(release_in, release_ref, local_sem.at[3]),
+            pltpu.make_async_copy(taps_in, taps_ref, local_sem.at[4]),
         )
 
     def remote(src, dst, send, recv, to_tm, to_slab):
@@ -99,28 +105,39 @@
         return (
             remote(decay_ref.at[pl.ds(local - SIDE, SIDE)], centre.at[pl.ds(0, SIDE)], side_send.at[0], side_recv.at[0], tm, other),
             remote(source_ref.at[0, pl.ds(local - SIDE, SIDE)], field.at[pl.ds(0, SIDE)], side_send.at[1], side_recv.at[1], tm, other),
-            remote(initial_ref.at[0, :, pl.ds(local - WIDE, WIDE)], start.at[:, pl.ds(0, WIDE)], side_send.at[2], side_recv.at[2], tm, other),
         )
 
     def to_low():
         other = slab - 1
         return (
-            remote(decay_ref.at[pl.ds(0, SIDE)], centre.at[pl.ds(SIDE + local, SIDE)], side_send.at[3], side_recv.at[3], tm, other),
-            remote(source_ref.at[0, pl.ds(0, SIDE)], field.at[pl.ds(SIDE + local, SIDE)], side_send.at[4], side_recv.at[4], tm, other),
-            remote(initial_ref.at[0, :, pl.ds(0, WIDE)], start.at[:, pl.ds(WIDE + local, WIDE)], side_send.at[5], side_recv.at[5], tm, other),
-        )
-
-    def observation(c):
-        return remote(observed_ref.at[0, c], target.at[c], obs_send.at[c], obs_recv.at[c], partner, slab)
-
-    def halo_high(c):
+            remote(decay_ref.at[pl.ds(0, SIDE)], centre.at[pl.ds(SIDE + local, SIDE)], side_send.at[2], side_recv.at[2], tm, other),
+            remote(source_ref.at[0, pl.ds(0, SIDE)], field.at[pl.ds(SIDE + local, SIDE)], side_send.at[3], side_recv.at[3], tm, other),
+        )
+
+    def span(g):
+        return pl.ds(g * GROUP, GROUP)
+
+    def start_high(g):
         return remote(
-            adjoint.at[c, pl.ds(local, SIDE)], adjoint.at[c, pl.ds(0, SIDE)], halo_send.at[0, c], halo_recv.at[0, c], tm, slab + 1
-        )
-
-    def halo_low(c):
+            initial_ref.at[0, span(g), pl.ds(local - WIDE, WIDE)], start.at[span(g), pl.ds(0, WIDE)], start_send.at[0, g], start_recv.at[0, g], tm, slab + 1
+        )
+
+    def start_low(g):
         return remote(
-            adjoint.at[c, pl.ds(SIDE, SIDE)], adjoint.at[c, pl.ds(SIDE + local, SIDE)], halo_send.at[1, c], halo_recv.at[1, c], tm, slab - 1
+            initial_ref.at[0, span(g), pl.ds(0, WIDE)], start.at[span(g), pl.ds(WIDE + local, WIDE)], start_send.at[1, g], start_recv.at[1, g], tm, slab - 1
+        )
+
+    def observation(g):
+        return remote(observed_ref.at[0, span(g)], target.at[span(g)], obs_send.at[g], obs_recv.at[g], partner, slab)
+
+    def halo_high(g):
+        return remote(
+            adjoint.at[span(g), pl.ds(local, SIDE)], adjoint.at[span(g), pl.ds(0, SIDE)], halo_send.at[0, g], halo_recv.at[0, g], tm, slab + 1
+        )
+
+    def halo_low(g):
+        return remote(
+            adjoint.at[span(g), pl.ds(SIDE, SIDE)], adjoint.at[span(g), pl.ds(SIDE + local, SIDE)], halo_send.at[1, g], halo_recv.at[1, g], tm, slab - 1
         )
 
     def turn(other):
@@ -164,9 +181,19 @@
         for copy in to_low():
             copy.start()
 
-    @pl.loop(1, channels)
-    def _(c):
-        observation(c).start()
+    @pl.loop(0, parcels)
+    def _(g):
+        @pl.when(has_high)
+        def _():
+            start_high(g).start()
+
+        @pl.when(has_low)
+        def _():
+            start_low(g).start()
+
+        @pl.when(g > 0)
+        def _():
+            observation(g).start()
 
     @pl.when(jnp.logical_not(has_low))
     def _():
@@ -184,6 +211,9 @@
 
     low = jnp.where(has_low, 1.0, 0.0).astype(jnp.float32)
     high = jnp.where(has_high, 1.0, 0.0).astype(jnp.float32)
+
+    for copy in local_copies():
+        copy.wait()
 
     taps = taps_ref.shape[0]
     offset = (
@@ -204,9 +234,6 @@
         for place in (x_at == 0, x_at == nx - 1, y_at == 0, y_at == ny - 1)
     )
 
-    for copy in local_copies():
-        copy.wait()
-
     @pl.when(has_low)
     def _():
         for copy in to_high():
@@ -219,8 +246,7 @@
 
     centre[...] = (1.0 - 2.0 * vertical_rate - 4.0 * lateral_rate) - centre[...]
 
-    @pl.loop(0, channels)
-    def _(c):
+    def forward(c):
         when = release_ref[tm, c]
         current = start[c]
         for step in range(STEPS):
@@ -232,7 +258,7 @@
                 current = inside(current, halo, low, high)
                 states[c, step] = current[halo:-halo]
             else:
-                final[c] = current
+                adjoint[c, pl.ds(SIDE, local)] = current
 
     def backward(c):
         when = release_ref[tm, c]
@@ -253,35 +279,50 @@
         total[0] = source_sum
         total[1] = decay_sum
 
-    def await_halo(c):
+    def members(g, action):
+        for c in range(GROUP):
+            action(g * GROUP + c)
+
+    def settle(g):
         @pl.when(has_low)
         def _():
-            halo_high(c).wait_recv()
+            halo_high(g).wait_recv()
 
         @pl.when(has_high)
         def _():
-            halo_low(c).wait_recv()
-
-    @pl.loop(0, channels)
-    def _(c):
-        observation(c).wait_recv()
-        adjoint[c, pl.ds(SIDE, local)] = final[c] - target[c]
+            halo_low(g).wait_recv()
+
+        members(g, backward)
+
+    @pl.loop(0, parcels)
+    def _(g):
+        @pl.when(has_low)
+        def _():
+            start_high(g).wait_recv()
 
         @pl.when(has_high)
         def _():
-            halo_high(c).start()
+            start_low(g).wait_recv()
+
+        members(g, forward)
+        observation(g).wait_recv()
+        adjoint[span(g), pl.ds(SIDE, local)] = adjoint[span(g), pl.ds(SIDE, local)] - target[span(g)]
+
+        @pl.when(has_high)
+        def _():
+            halo_high(g).start()
 
         @pl.when(has_low)
         def _():
-            halo_low(c).start()
-
-        @pl.when(c > 0)
-        def _():
-            await_halo(c - 1)
-            backward(c - 1)
-
-    await_halo(channels - 1)
-    backward(channels - 1)
+            halo_low(g).start()
+
+        @pl.when(g >= LAG)
+        def _():
+            settle(g - LAG)
+
+    @pl.loop(parcels - LAG, parcels)
+    def _(g):
+        settle(g)
 
     for kind in range(2):
         turned[kind] = jnp.swapaxes(total[kind], 0, 1)
@@ -300,17 +341,19 @@
         for copy in to_low():
             copy.wait_send()
 
-    @pl.loop(0, channels)
-    def _(c):
-        observation(c).wait_send()
+    @pl.loop(0, parcels)
+    def _(g):
+        observation(g).wait_send()
 
         @pl.when(has_high)
         def _():
-            halo_high(c).wait_send()
+            halo_high(g).wait_send()
+            start_high(g).wait_send()
 
         @pl.when(has_low)
         def _():
-            halo_low(c).wait_send()
+            halo_low(g).wait_send()
+            start_low(g).wait_send()
 
     @pl.loop(0, slabs)
     def _(other):
@@ -323,20 +366,24 @@
             other,
         ).wait_recv()
 
+    @pl.loop(0, slabs)
+    def _(other):
+        turn(other).wait_send()
+
+
+def smooth(slabs, columns, matrix, source_out, decay_out):
+    slab = lax.axis_index("slab")
+    _, rows, _, nx = columns.shape
+    width = source_out.shape[2]
     for kind, out in enumerate((source_out, decay_out)):
         for row in range(rows):
-            smooth = jnp.dot(
+            result = jnp.dot(
                 matrix[...], columns[kind, row], precision=lax.Precision.HIGHEST, preferred_element_type=jnp.float32
             )
             if width < nx:
-                smooth = pltpu.roll(smooth, lax.rem(nx - lax.rem(slab * width, nx), nx), axis=1)[:, :width]
-                out[0] = smooth
+                out[0] = pltpu.roll(result, lax.rem(nx - lax.rem(slab * width, nx), nx), axis=1)[:, :width]
             else:
-                out[0, :, pl.ds(row * nx, nx)] = smooth
-
-    @pl.loop(0, slabs)
-    def _(other):
-        turn(other).wait_send()
+                out[0, :, pl.ds(row * nx, nx)] = result
 
 
 def solution(mesh):
@@ -359,40 +406,47 @@
         assert width % nx == 0 or nx % width == 0
         f32 = jnp.float32
         anywhere = pl.BlockSpec(memory_space=pl.ANY)
-        scalars = pl.BlockSpec(memory_space=pltpu.SMEM)
         out = jax.ShapeDtypeStruct((1, depth, width), f32)
         dma = pltpu.SemaphoreType.DMA
-        return pl.pallas_call(
+        columns, matrix = pl.pallas_call(
             functools.partial(kernel, groups, slabs),
-            out_shape=(out, out),
-            in_specs=[scalars, scalars] + [anywhere] * 4,
-            out_specs=[pl.BlockSpec(memory_space=pltpu.VMEM)] * 2,
+            out_shape=(
+                jax.ShapeDtypeStruct((2, rows, depth, nx), f32),
+                jax.ShapeDtypeStruct((depth, depth), f32),
+            ),
+            in_specs=[anywhere] * 6,
+            out_specs=[anywhere, pl.BlockSpec(memory_space=pltpu.VMEM)],
             scratch_shapes=[
                 pltpu.VMEM((channels, local + 2 * WIDE, ny, nx), f32),
                 pltpu.VMEM((local + 2 * SIDE, ny, nx), f32),
                 pltpu.VMEM((local + 2 * SIDE, ny, nx), f32),
                 pltpu.VMEM((channels, STEPS - 1, local, ny, nx), f32),
                 pltpu.VMEM((channels, local, ny, nx), f32),
-                pltpu.VMEM((channels, local, ny, nx), f32),
                 pltpu.VMEM((channels, local + 2 * SIDE, ny, nx), f32),
                 pltpu.VMEM((2, local, ny, nx), f32),
                 pltpu.VMEM((2, ny, local, nx), f32),
-                pltpu.VMEM((2, rows, depth, nx), f32),
-                pltpu.VMEM((depth, depth), f32),
-                dma((3,)),
-                dma((6,)),
-                dma((6,)),
-                dma((channels,)),
-                dma((channels,)),
-                dma((2, channels)),
-                dma((2, channels)),
+                pltpu.SMEM(release.shape, jnp.int32),
+                pltpu.SMEM(smooth_taps.shape, f32),
+                dma((5,)),
+                dma((4,)),
+                dma((4,)),
+                dma((2, channels // GROUP)),
+                dma((2, channels // GROUP)),
+                dma((channels // GROUP,)),
+                dma((channels // GROUP,)),
+                dma((2, channels // GROUP)),
+                dma((2, channels // GROUP)),
                 dma((slabs,)),
                 dma((slabs,)),
             ],
             compiler_params=pltpu.CompilerParams(
-                collective_id=0, has_side_effects=True, vmem_limit_bytes=40 * 1024 * 1024
+                collective_id=0, has_side_effects=True, vmem_limit_bytes=60 * 1024 * 1024
             ),
         )(release, smooth_taps, initial, source, decay_rate, observed)
+        vmem = pl.BlockSpec(memory_space=pltpu.VMEM)
+        return pl.pallas_call(
+            functools.partial(smooth, slabs), out_shape=(out, out), in_specs=[vmem, vmem], out_specs=[vmem, vmem]
+        )(columns, matrix)
 
     return jax.shard_map(
         body,

time: 57.3 us -> 42 us (0.73)
  Pallas kernels: 49.6 us -> 41.2 us
  local copies, waits for them, and re-layouts: 6.72 us -> 0 us
    pallas_call x1 -> x2, Pallas kernels: 49.6 us -> 41.2 us  [the longest x1 39.4 us: body(): pl.pallas_call(functools.partial(kernel, groups, slabs), out_shape=(jax.S...]
    unnamed x14 -> x0, local copies, waits for them, and re-layouts: 6.72 us -> none
where the time goes in v2:
time: 42 us; the launch traced here: 41.8 us
  Pallas kernels  41.2 us (98%)
  between operations  0.64 us (2%)
    pallas_call x1, Pallas kernels, body(): pl.pallas_call(functools.partial(kernel, groups, slabs), out_shape=(jax.S...  39.4 us
    pallas_call x1, Pallas kernels, body(): pl.pallas_call(functools.partial(smooth, slabs), out_shape=(out, out), in...  1.78 us

profile of v2, /device:TPU:0, one launch (start us, length us, event | category | flops | bytes accessed | tf_op | source)
XLA Modules:
  0.0 41.8 jit_solution(69851442578921346)
XLA Ops:
  0.6 39.4 %shard_map.77 = (f32[2,2,64,128]{3,2,1,0:T(8,128)}, f32[64,64]{1,0:T(8,128)}) custom-call(s32[4,16]{1,0:T(4,128)} %release_in.1, f32[31]{0:T(128)} %taps_in.1, f32[1,16,8,16,128]{4,3,2,1,0:T(8,128)} %initial_ref.1, f32[1,8,16,128]{3,2,1,0:T(8,128)} %source_ref.1, f32[8,16,128]{2,1,0:T(8,128)} %decay_ref.1, f32[1,16,8,16,128]{4,3,2,1,0:T(8,128)} %observed_ref.1), custom_call_target="tpu_custom_call" | custom-call | tf_op jit(solution)/shard_map/pallas_call | solution.py:411
  40.1 1.8 %shard_map.78 = (f32[1,64,256]{2,1,0:T(8,128)}, f32[1,64,256]{2,1,0:T(8,128)}) custom-call(f32[2,2,64,128]{3,2,1,0:T(8,128)} %get-tuple-element.4.columns, f32[64,64]{1,0:T(8,128)} %get-tuple-element.5.matrix), custom_call_target="tpu_custom_call" | custom-call | tf_op jit(solution)/shard_map/pallas_call | solution.py:447

commit v3 on v2

--- a/solution.py
+++ b/solution.py
@@ -375,15 +375,18 @@
     slab = lax.axis_index("slab")
     _, rows, _, nx = columns.shape
     width = source_out.shape[2]
+    pieces = [columns[kind, row] for kind in range(2) for row in range(rows)]
+    result = jnp.dot(
+        matrix[...],
+        jnp.concatenate(pieces, axis=1),
+        precision=lax.Precision.HIGHEST,
+        preferred_element_type=jnp.float32,
+    )
     for kind, out in enumerate((source_out, decay_out)):
-        for row in range(rows):
-            result = jnp.dot(
-                matrix[...], columns[kind, row], precision=lax.Precision.HIGHEST, preferred_element_type=jnp.float32
-            )
-            if width < nx:
-                out[0] = pltpu.roll(result, lax.rem(nx - lax.rem(slab * width, nx), nx), axis=1)[:, :width]
-            else:
-                out[0, :, pl.ds(row * nx, nx)] = result
+        part = result[:, kind * rows * nx : (kind + 1) * rows * nx]
+        if width < nx:
+            part = pltpu.roll(part, lax.rem(nx - lax.rem(slab * width, nx), nx), axis=1)[:, :width]
+        out[0] = part
 
 
 def solution(mesh):

time: 42 us -> 42 us (level)
  no operation moved by 1% of the time
where the time goes in v3:
time: 42 us; the launch traced here: 41.9 us
  Pallas kernels  41.2 us (98%)
  between operations  0.64 us (2%)
    pallas_call x1, Pallas kernels, body(): pl.pallas_call(functools.partial(kernel, groups, slabs), out_shape=(jax.S...  39.4 us
    pallas_call x1, Pallas kernels, body(): pl.pallas_call(functools.partial(smooth, slabs), out_shape=(out, out), in...  1.81 us

profile of v3, /device:TPU:0, one launch (start us, length us, event | category | flops | bytes accessed | tf_op | source)
XLA Modules:
  0.0 41.9 jit_solution(14161766145454926616)
XLA Ops:
  0.6 39.4 %shard_map.77 = (f32[2,2,64,128]{3,2,1,0:T(8,128)}, f32[64,64]{1,0:T(8,128)}) custom-call(s32[4,16]{1,0:T(4,128)} %release_in.1, f32[31]{0:T(128)} %taps_in.1, f32[1,16,8,16,128]{4,3,2,1,0:T(8,128)} %initial_ref.1, f32[1,8,16,128]{3,2,1,0:T(8,128)} %source_ref.1, f32[8,16,128]{2,1,0:T(8,128)} %decay_ref.1, f32[1,16,8,16,128]{4,3,2,1,0:T(8,128)} %observed_ref.1), custom_call_target="tpu_custom_call" | custom-call | tf_op jit(solution)/shard_map/pallas_call | solution.py:414
  40.1 1.8 %shard_map.78 = (f32[1,64,256]{2,1,0:T(8,128)}, f32[1,64,256]{2,1,0:T(8,128)}) custom-call(f32[2,2,64,128]{3,2,1,0:T(8,128)} %get-tuple-element.4.columns, f32[64,64]{1,0:T(8,128)} %get-tuple-element.5.matrix), custom_call_target="tpu_custom_call" | custom-call | tf_op jit(solution)/shard_map/pallas_call | solution.py:450
